TPU v7x, 32 devices: a whole 2x2x4 slice. The times are simulated.
32 devices in a mesh: seq: 4 (over y, core), chan: 8 (over z, x).
Axes of the slice: x: 2, y: 2, z: 4, core: 2. Of those that a mesh axis runs over, the one named last changes fastest.
Arguments:
- query_rows: bfloat16 [512, 8192], P('seq', 'chan'), may hold values from -6 to 6
- key_rows: bfloat16 [512, 8192], P('seq', 'chan'), may hold values from -6 to 6
- value_rows: bfloat16 [512, 8192], P('seq', 'chan'), may hold values from -6 to 6
- short_taps: float32 [3, 3, 8192], P(None, None, 'chan'), may hold values from -3.5 to 3.5
- long_filter: float32 [512, 128], P('seq'), may hold values from -1.1 to 1.1
- cotangent: bfloat16 [512, 8192], P('seq', 'chan'), may hold values from -6 to 6
Outputs:
- hyena_out: bfloat16 [512, 8192], P('seq', 'chan')
- grad_query: bfloat16 [512, 8192], P('seq', 'chan')
- grad_key: bfloat16 [512, 8192], P('seq', 'chan')
- grad_value: bfloat16 [512, 8192], P('seq', 'chan')
- grad_filter: float32 [512, 128], P('seq')
All inputs are finite; a program needn't handle non-finite values.
Results may differ from a plain program's by a relative error of at most 0.001.
Values may be sent and summed in bfloat16 or wider, within the bound.
No kernel may reach another device: no remote copies, remote signals or barrier semaphores. Data moves between devices by JAX's collectives and lax.ppermute only.
A program may use at most 64 MiB of HBM per device.

v0:
```python
import functools

import jax
import jax.numpy as jnp
import ml_dtypes
import numpy as np
from jax import lax
from jax.experimental import pallas as pl
from jax.experimental.pallas import tpu as pltpu
from jax.sharding import PartitionSpec as P

F32 = jnp.float32
BF16 = jnp.bfloat16
EDGE = 8
HEAD = 16
VMEM = pl.BlockSpec(memory_space=pltpu.VMEM)
HBM = pl.BlockSpec(memory_space=pltpu.HBM)


def split_table(table):
    high = table.astype(ml_dtypes.bfloat16)
    low = (table - high.astype(np.float64)).astype(ml_dtypes.bfloat16)
    return high, low


def dft_tables(length):
    frequency = np.pi * (2 * np.arange(length) + 1) / (2 * length)
    into = frequency[:, None] * np.arange(length)[None, :]
    high, low = split_table(np.concatenate([np.cos(into), -np.sin(into)], axis=0))
    forward = np.concatenate([high, high, low], axis=1)
    forward = np.pad(forward, ((0, EDGE), (0, 0)))
    back = np.arange(length + EDGE)[:, None] * frequency[None, :]
    high, low = split_table(np.concatenate([np.cos(back), -np.sin(back)], axis=1) / length)
    inverse = np.concatenate([high, high, low], axis=1)
    return jnp.asarray(forward), jnp.asarray(inverse)


def halves(values):
    high = values.astype(BF16)
    return high, (values - high.astype(F32)).astype(BF16)


def table_dot(table, values):
    high, low = halves(values)
    return jnp.dot(
        table, jnp.concatenate([high, low, high], axis=0), preferred_element_type=F32
    )


def tap_sum(rows_ref, first, count, weights):
    total = weights[0:1] * rows_ref[first : first + count]
    for shift in range(1, weights.shape[0]):
        total = total + weights[shift : shift + 1] * rows_ref[first - shift : first - shift + count]
    return total


def put_filter(unit, first, filter_high, filter_low):
    length, groups = filter_high.shape
    width = unit.shape[1]
    rows = length * groups // width
    for tile in range(width // groups):
        lanes = slice(tile * groups, (tile + 1) * groups)
        part = slice(tile * rows, (tile + 1) * rows)
        unit[first : first + rows, lanes] = filter_high[part]
        unit[first + rows : first + 2 * rows, lanes] = filter_low[part]


def get_filter(unit, first, length, groups):
    width = unit.shape[1]
    rows = length * groups // width
    pieces = []
    for tile in range(width // groups):
        lanes = slice(tile * groups, (tile + 1) * groups)
        pieces.append(
            unit[first : first + rows, lanes].astype(F32)
            + unit[first + rows : first + 2 * rows, lanes].astype(F32)
        )
    return jnp.concatenate(pieces, axis=0)


def fetch_kernel(q_hbm, k_hbm, v_hbm, c_hbm, *refs):
    others = refs[:4]
    rows_ref, marks_ref, *other_refs = refs[4:10]
    edge, sems = refs[10:]
    length = q_hbm.shape[0]
    copies = [
        pltpu.make_async_copy(source, rows_ref.at[index], sems.at[index])
        for index, source in enumerate((q_hbm, k_hbm, v_hbm, c_hbm))
    ]
    copies += [
        pltpu.make_async_copy(source, target, sems.at[4 + index])
        for index, (source, target) in enumerate(zip(others, other_refs))
    ]
    for copy in copies:
        copy.start()
    for copy in copies[:4]:
        copy.wait()
    margin = others[0].shape[1] - 1
    edge[...] = jnp.zeros(edge.shape, F32)
    for p in range(4):
        first = rows_ref[p, 0:HEAD].astype(F32)
        edge[(3 + p) * margin : (4 + p) * margin] = first[0:margin]
        if p < 3:
            last = rows_ref[p, length - HEAD :].astype(F32)
            edge[p * margin : (p + 1) * margin] = last[HEAD - margin :]
    marks_ref[...] = edge[...].astype(BF16)
    for copy in copies[4:]:
        copy.wait()


def own_kernel(bits, tile_width, rows_ref, taps_ref, filter_ref, pair_ref, conv_ref, *refs):
    unit_refs, window = refs[:-1], refs[-1]
    length, width = rows_ref.shape[1:]
    half = width // 2
    me = lax.axis_index("seq")
    filter_high, filter_low = halves(filter_ref[...])
    put_filter(pair_ref, 4 * length, filter_high, filter_low)
    for later in unit_refs[1::2]:
        put_filter(later, 2 * length, filter_high, filter_low)
    window[:, 0:EDGE] = jnp.zeros((3, EDGE, tile_width), F32)
    for tile in range(width // tile_width):
        lanes = slice(tile * tile_width, (tile + 1) * tile_width)
        convs = []
        for p in range(3):
            window[p, EDGE:] = rows_ref[p, :, lanes].astype(F32)
            conv = tap_sum(window.at[p], EDGE, length, taps_ref[p, :, lanes])
            conv_ref[p, :, lanes] = conv
            convs.append(conv)
        incoming = rows_ref[3, :, lanes].astype(F32)
        parts = [*halves(convs[1] * convs[2]), *halves(incoming * convs[0])]
        for index, part in enumerate(parts):
            pair_ref[index * length : (index + 1) * length, lanes] = part
        in_half = tile * tile_width // half
        lanes_half = slice(tile * tile_width % half, tile * tile_width % half + tile_width)
        for index, bit in enumerate(bits):
            low_side = (me // bit) % 2 == 0
            first, later = unit_refs[2 * index : 2 * index + 2]
            target_low, target_high = (first, later) if in_half == 0 else (later, first)

            @pl.when(low_side)
            def _():
                target_low[0:length, lanes_half] = parts[0]
                target_low[length : 2 * length, lanes_half] = parts[1]

            @pl.when(jnp.logical_not(low_side))
            def _():
                target_high[0:length, lanes_half] = parts[2]
                target_high[length : 2 * length, lanes_half] = parts[3]


def first_kernel(marks_refs, taps_ref, own_marks, *refs):
    arrived = refs[:marks_refs]
    firsts_ref, conv_ref, after_ref, marks, convs, window = refs[marks_refs:]
    blocks = firsts_ref.shape[0]
    me = lax.axis_index("seq")
    margin = taps_ref.shape[1] - 1
    nothing = jnp.zeros(marks.shape[1:], F32)
    marks[0] = nothing
    marks[blocks + 1] = nothing
    marks[me + 1] = own_marks[...].astype(F32)
    index = 1
    for ref in arrived:
        for place in range(ref.shape[0] // HEAD):
            marks[(me ^ index_of(index, blocks)) + 1] = ref[
                place * HEAD : (place + 1) * HEAD
            ].astype(F32)
            index += 1
    window[...] = jnp.zeros(window.shape, F32)
    convs[blocks] = jnp.zeros(convs.shape[1:], F32)
    for block in range(blocks):
        for p in range(3):
            window[EDGE - margin : EDGE] = marks[block, p * margin : (p + 1) * margin]
            window[EDGE : EDGE + margin] = marks[block + 1, (3 + p) * margin : (4 + p) * margin]
            convs[block, p] = tap_sum(window, EDGE, EDGE, taps_ref[p])
        window[EDGE : EDGE + margin] = marks[block + 1, 6 * margin : 7 * margin]
        firsts_ref[block, 0] = convs[block, 1] * convs[block, 2]
        firsts_ref[block, 1] = window[EDGE:] * convs[block, 0]
    conv_ref[...] = convs[me]
    after_ref[0:2] = convs[me + 1, 1:3]
    window[EDGE : EDGE + margin] = marks[me + 2, 6 * margin : 7 * margin]
    after_ref[2] = window[EDGE:]


def index_of(count, blocks):
    order, bit = [0], blocks // 2
    while bit:
        order += [index ^ bit for index in order]
        bit //= 2
    return order[count]


def with_first(margin, first, rows):
    true = jnp.concatenate([first, jnp.zeros((HEAD - EDGE, first.shape[1]), F32)], axis=0)
    row = lax.broadcasted_iota(jnp.int32, true.shape, 0)
    return jnp.where(row < margin, true, rows)


def spectrum(forward, margin, first, ref, place, lanes):
    length = forward.shape[1] // 3
    parts = []
    for index, part in enumerate(halves(first)):
        begin = place + index * length
        head = with_first(margin, part.astype(F32), ref[begin : begin + HEAD, lanes].astype(F32))
        parts += [head.astype(BF16), ref[begin + HEAD : begin + length, lanes]]
    return jnp.dot(
        forward, jnp.concatenate([*parts, *parts[0:2]], axis=0), preferred_element_type=F32
    )


def cross_add(cross, distance, early, late, groups):
    length = early.shape[0] // 2
    e_re, e_im = early[0:length], early[length:]
    l_re, l_im = late[0:length], late[length:]
    re = e_re * l_re + e_im * l_im
    im = e_re * l_im - e_im * l_re
    parts = range(early.shape[1] // groups)
    cross[distance, 0:length] += sum(re[:, p * groups : (p + 1) * groups] for p in parts)
    cross[distance, length:] += sum(im[:, p * groups : (p + 1) * groups] for p in parts)


def chip_kernel(
    tile_width,
    groups,
    margin,
    own_ref,
    other_ref,
    firsts_ref,
    forward_ref,
    spec_ref,
    cross_ref,
):
    length = forward_ref.shape[1] // 3
    width = own_ref.shape[1]
    me = lax.axis_index("seq")
    core = me % 2
    forward = forward_ref[0 : 2 * length]
    cross_ref[...] = jnp.zeros(cross_ref.shape, F32)

    def one_tile(step, carry):
        lanes = pl.ds(pl.multiple_of(step * tile_width, tile_width), tile_width)
        for ref, slot, block in ((own_ref, core, me), (other_ref, 1 - core, me ^ 1)):
            for kind in range(2):
                first = firsts_ref[block, kind, :, lanes]
                spec_ref[2 * kind + slot, :, lanes] = spectrum(
                    forward, margin, first, ref, 2 * kind * length, lanes
                )
        cross_add(cross_ref, 0, spec_ref[core, :, lanes], spec_ref[2 + core, :, lanes], groups)

        @pl.when(2 * step * tile_width // width == core)
        def _():
            cross_add(cross_ref, 1, spec_ref[0, :, lanes], spec_ref[3, :, lanes], groups)

        return carry

    lax.fori_loop(0, width // tile_width, one_tile, 0)


def filter_grad_kernel(
    blocks,
    tile_width,
    margin,
    spec_ref,
    near_ref,
    firsts_ref,
    forward_ref,
    inverse_ref,
    *refs,
):
    chips = blocks // 2
    units = refs[: chips - 1]
    gf_refs, cross = refs[chips - 1 : -1], refs[-1]
    length = forward_ref.shape[1] // 3
    groups = near_ref.shape[2]
    half = spec_ref.shape[2] // 2
    me = lax.axis_index("seq")
    core, chip = me % 2, me // 2
    forward = forward_ref[0 : 2 * length]
    cross[0:2] = near_ref[...]
    cross[2:] = jnp.zeros((blocks - 1, 2 * length, groups), F32)
    for index, unit in enumerate(units):
        other = chip ^ (index + 1)

        def one_tile(step, carry):
            start = pl.multiple_of(step * tile_width, tile_width)
            lanes = pl.ds(start, tile_width)
            kind = jnp.where(other < chip, 0, 1)
            wide_lanes = pl.ds(pl.multiple_of(kind * half + start, tile_width), tile_width)
            first = firsts_ref[2 * other + core, kind, :, wide_lanes]
            spec = spectrum(forward, margin, first, unit, 0, lanes)

            @pl.when(other < chip)
            def _():
                for slot in range(2):
                    distance = 2 * chip + slot - (2 * other + core)
                    cross_add(cross, distance, spec, spec_ref[2 + slot, :, wide_lanes], groups)

            @pl.when(other > chip)
            def _():
                for slot in range(2):
                    distance = 2 * other + core - (2 * chip + slot)
                    cross_add(cross, distance, spec_ref[slot, :, wide_lanes], spec, groups)

            return carry

        lax.fori_loop(0, half // tile_width, one_tile, 0)

    inverse = inverse_ref[0:length]
    sign = signs(length, groups)
    for parity, ref in zip((1, 0), gf_refs):
        for place in range(blocks // 2):
            block = me ^ (2 * place + parity)
            re = cross[block, 0:length] + sign * cross[block + 1, length:]
            im = cross[block, length:] - sign * cross[block + 1, 0:length]
            ref[place] = table_dot(inverse, jnp.concatenate([re, im], axis=0))


def signs(length, groups):
    row = lax.broadcasted_iota(jnp.int32, (length, groups), 0)
    return jnp.where(row % 2 == 0, 1.0, -1.0)


def result_kernel(blocks, tile_width, stage, *refs):
    others = blocks // 2 - 1
    (
        rows_ref,
        taps_ref,
        filter_ref,
        conv_ref,
        conv_first,
        firsts_ref,
        after_ref,
        other_ref,
        spec_ref,
        forward_ref,
        inverse_ref,
    ) = refs[:11]
    refs = refs[11:]
    units = [refs[4 * index : 4 * index + 4] for index in range(others)]
    refs = refs[4 * others :]
    if stage == 0:
        outs, (spectra, filter_rows) = refs[:4], refs[4:6]
        refs = refs[6:]
    else:
        spectra, filter_rows = refs[:2]
        outs = refs[6:10]
        refs = refs[10:]
    acc, fix, grads, rows_out, sems = refs
    length, width = rows_ref.shape[1:]
    groups = filter_ref.shape[1]
    half = width // 2
    margin = taps_ref.shape[1] - 1
    me = lax.axis_index("seq")
    core, chip = me % 2, me // 2
    forward, inverse = forward_ref[0 : 2 * length], inverse_ref[...]

    if stage == 0:
        sign = signs(length, groups)
        for edge in (0, 1, blocks + 2):
            filter_rows[edge] = jnp.zeros((length, groups), F32)
        filter_rows[me + 2] = filter_ref[...]
        filter_rows[(me ^ 1) + 2] = get_filter(other_ref, 4 * length, length, groups)
        for index, unit in enumerate(units):
            block = me ^ (2 * (index + 1))
            filter_rows[block + 2] = get_filter(unit[1], 2 * length, length, groups)
            filter_rows[(block ^ 1) + 2] = get_filter(unit[3], 2 * length, length, groups)
        previous = None
        for distance in range(blocks):
            own = table_dot(forward, filter_rows[distance + 2])
            if previous is None:
                spectra[distance] = own
            else:
                spectra[distance, 0:length] = own[0:length] - sign * previous[length:]
                spectra[distance, length:] = own[length:] + sign * previous[0:length]
            previous = own

    def wide(values):
        return jnp.concatenate([values] * (tile_width // groups), axis=1)

    def filter_row(block, row):
        return wide(filter_rows[block + 2, pl.ds(row, 1)])

    def add_lower(distance, signal, spec, fresh=False):
        re, im = spec[0:length], spec[length:]
        h_re, h_im = wide(spectra[distance, 0:length]), wide(spectra[distance, length:])
        new_re = h_re * re - h_im * im
        new_im = h_re * im + h_im * re
        acc[0, 0:length] = new_re if fresh else acc[0, 0:length] + new_re
        acc[0, length:] = new_im if fresh else acc[0, length:] + new_im
        near = filter_row(distance + 1, 0) + filter_row(distance - 1, 0)
        far = filter_row(distance + 1, 1) + filter_row(distance - 1, 1)
        fix[0:1] += signal[0:1] * near
        fix[1:2] += signal[0:1] * far + signal[1:2] * near

    def add_upper(distance, signal, spec, fresh=False):
        re, im = spec[0:length], spec[length:]
        h_re, h_im = wide(spectra[distance, 0:length]), wide(spectra[distance, length:])
        new_re = h_re * re + h_im * im
        new_im = h_re * im - h_im * re
        acc[1, 0:length] = new_re if fresh else acc[1, 0:length] + new_re
        acc[1, length:] = new_im if fresh else acc[1, length:] + new_im
        fix[EDGE + 1 : EDGE + 2] += signal[0:1] * (
            filter_row(distance - 2, length - 1) + filter_row(distance, length - 1)
        )

    copies = []
    for tile in range(half // tile_width):
        start = stage * half + tile * tile_width
        lanes = slice(start, start + tile_width)
        lanes_half = slice(tile * tile_width, (tile + 1) * tile_width)
        weights = [taps_ref[p, :, lanes] for p in range(3)]
        fix[...] = jnp.zeros(fix.shape, F32)

        add_lower(0, firsts_ref[me, 0, :, lanes], spec_ref[core, :, lanes], True)
        add_upper(0, firsts_ref[me, 1, :, lanes], spec_ref[2 + core, :, lanes], True)

        @pl.when(core == 1)
        def _():
            add_lower(1, firsts_ref[me - 1, 0, :, lanes], spec_ref[0, :, lanes])

        @pl.when(core == 0)
        def _():
            add_upper(1, firsts_ref[me + 1, 1, :, lanes], spec_ref[3, :, lanes])

        for index, unit in enumerate(units):
            other = chip ^ (index + 1)
            for side in range(2):
                first, later = unit[2 * side : 2 * side + 2]
                body_low, body_high = (first, later) if stage == 0 else (later, first)
                block = 2 * other + (core if side == 0 else 1 - core)

                @pl.when(other < chip)
                def _():
                    signal = firsts_ref[block, 0, :, lanes]
                    spec = spectrum(forward, margin, signal, body_low, 0, lanes_half)
                    add_lower(me - block, signal, spec)

                @pl.when(other > chip)
                def _():
                    signal = firsts_ref[block, 1, :, lanes]
                    spec = spectrum(forward, margin, signal, body_high, 0, lanes_half)
                    add_upper(block - me, signal, spec)

        after_key, after_value, after_incoming = [
            after_ref[p, :, lanes][0:margin] for p in range(3)
        ]
        gated = after_key * after_value
        zero_lag, one_lag = filter_row(0, 0), filter_row(0, 1)
        fix[0:1] += gated[0:1] * zero_lag
        fix[1:2] += gated[1:2] * zero_lag + gated[0:1] * one_lag

        long_conv = table_dot(inverse, acc[0])
        gated_grad = table_dot(inverse, acc[1])
        query_conv, key_conv, value_conv = [
            jnp.concatenate(
                [
                    with_first(margin, conv_first[p, :, lanes], conv_ref[p, 0:HEAD, lanes]),
                    conv_ref[p, HEAD:, lanes],
                ],
                axis=0,
            )
            for p in range(3)
        ]
        incoming = rows_ref[3, :, lanes].astype(F32)
        beyond = slice(length, length + margin)
        grad_edge = gated_grad[beyond] + fix[EDGE : EDGE + margin]
        grads[0, 0:length] = incoming * long_conv[0:length]
        grads[0, beyond] = after_incoming * (long_conv[beyond] + fix[0:margin])
        grads[1, 0:length] = gated_grad[0:length] * value_conv
        grads[1, beyond] = grad_edge * after_value
        grads[2, 0:length] = gated_grad[0:length] * key_conv
        grads[2, beyond] = grad_edge * after_key
        rows_out[0, :, lanes_half] = (query_conv * long_conv[0:length]).astype(BF16)
        for p in range(3):
            total = weights[p][0:1] * grads[p, 0:length]
            for shift in range(1, margin + 1):
                total = total + weights[p][shift : shift + 1] * grads[p, shift : shift + length]
            rows_out[1 + p, :, lanes_half] = total.astype(BF16)
        for p, out in enumerate(outs):
            copy = pltpu.make_async_copy(
                rows_out.at[p, :, lanes_half], out.at[:, lanes], sems.at[4 * tile + p]
            )
            copy.start()
            copies.append(copy)
    for copy in copies:
        copy.wait()


def per_device(query_rows, key_rows, value_rows, short_taps, long_filter, cotangent):
    length, width = query_rows.shape
    groups = long_filter.shape[1]
    blocks = lax.axis_size("seq")
    chans = lax.axis_size("chan")
    chips, half = blocks // 2, width // 2
    margin = short_taps.shape[1] - 1
    tile_width = min(half, 256)
    tiles = half // tile_width
    bits = []
    while 2 << len(bits) < blocks:
        bits.append(2 << len(bits))
    bits.reverse()
    forward, inverse = dft_tables(length)
    shape = jax.ShapeDtypeStruct

    def swap(block, bit):
        return lax.ppermute(block, "seq", [(i, i ^ bit) for i in range(blocks)])

    def call(kernel, outs, args, scratch, in_specs=None, out_specs=None, aliases={}, cost=1):
        return list(
            pl.pallas_call(
                kernel,
                out_shape=outs,
                in_specs=in_specs or [VMEM] * len(args),
                out_specs=out_specs or [VMEM] * len(outs),
                scratch_shapes=scratch,
                input_output_aliases=aliases,
                compiler_params=pltpu.CompilerParams(vmem_limit_bytes=40 * 1024 * 1024),
                cost_estimate=pl.CostEstimate(flops=1, bytes_accessed=cost, transcendentals=0),
            )(*args)
        )

    def after(value, *others):
        return lax.optimization_barrier((value, *others))[0]

    rows, marks, short_taps, long_filter, forward, inverse = call(
        fetch_kernel,
        [
            shape((4, length, width), BF16),
            shape((HEAD, width), BF16),
            shape(short_taps.shape, F32),
            shape(long_filter.shape, F32),
            shape(forward.shape, BF16),
            shape(inverse.shape, BF16),
        ],
        [
            pltpu.with_memory_space_constraint(array, pltpu.HBM)
            for array in (
                query_rows,
                key_rows,
                value_rows,
                cotangent,
                short_taps,
                long_filter,
                forward,
                inverse,
            )
        ],
        [pltpu.VMEM((HEAD, width), F32), pltpu.SemaphoreType.DMA((8,))],
        [HBM] * 8,
    )
    all_marks = []
    for bit in bits + [1]:
        all_marks.append(swap(jnp.concatenate([marks] + all_marks, axis=0), bit))
    firsts_true, conv_first, after_rows = call(
        functools.partial(first_kernel, len(all_marks)),
        [
            shape((blocks, 2, EDGE, width), F32),
            shape((3, EDGE, width), F32),
            shape((3, EDGE, width), F32),
        ],
        [short_taps, marks, *all_marks],
        [
            pltpu.VMEM((blocks + 2, HEAD, width), F32),
            pltpu.VMEM((blocks + 1, 3, EDGE, width), F32),
            pltpu.VMEM((2 * EDGE, width), F32),
        ],
    )
    filter_rows = length * groups // width
    pair_shape = shape((4 * length + 2 * filter_rows, width), BF16)
    first_shape = shape((2 * length, half), BF16)
    later_shape = shape((2 * length + 4 * filter_rows, half), BF16)
    pair, conv, *own_units = call(
        functools.partial(own_kernel, bits, tile_width),
        [pair_shape, shape((3, length, width), F32)] + [first_shape, later_shape] * len(bits),
        [rows, short_taps, long_filter],
        [pltpu.VMEM((3, EDGE + length, tile_width), F32)],
    )

    def gather(own):
        units = {}
        for bit, block in zip(bits, own):
            arrived = {bit // 2: swap(block, bit)}
            for index, unit in units.items():
                arrived[index ^ bit // 2] = swap(unit, bit)
            units.update(arrived)
        return [units[index] for index in range(1, chips)]

    firsts = gather([after(unit, all_marks[0]) for unit in own_units[0::2]])
    sibling = swap(pair, 1)
    laters = gather(own_units[1::2])
    spec, near = call(
        functools.partial(chip_kernel, tile_width, groups, margin),
        [shape((4, 2 * length, width), F32), shape((2, 2 * length, groups), F32)],
        [pair, sibling, firsts_true, forward],
        [],
    )
    odd, even = call(
        functools.partial(filter_grad_kernel, blocks, tile_width, margin),
        [shape((blocks // 2, length, groups), F32)] * 2,
        [spec, near, firsts_true, forward, inverse, *firsts],
        [pltpu.VMEM((blocks + 1, 2 * length, groups), F32)],
    )
    even = even + swap(odd, 1)
    step = 1
    if chans > 1:
        even = even + lax.ppermute(even, "chan", [(i, i ^ 1) for i in range(chans)])
        step = 2
    even = after(even, *laters)
    units = []
    for first, later in zip(firsts, laters):
        units += [first, later, swap(after(first, even), 1), swap(after(later, even), 1)]
    for bit in reversed(bits):
        arrived = swap(even[1::2], bit)
        even = even[0::2] + arrived
    grad_filter = even[0]

    rows_out = shape((length, width), BF16)
    windows = [
        shape((blocks, 2 * length, groups), F32),
        shape((blocks + 3, length, groups), F32),
    ]

    def results(stage, extra, outs, out_specs):
        args = [rows, short_taps, long_filter, conv, conv_first, firsts_true, after_rows]
        args += [sibling, spec, forward, inverse, *units]
        count = len(args)
        return call(
            functools.partial(result_kernel, blocks, tile_width, stage),
            outs,
            args + extra,
            [
                pltpu.VMEM((2, 2 * length, tile_width), F32),
                pltpu.VMEM((2 * EDGE, tile_width), F32),
                pltpu.VMEM((3, length + EDGE, tile_width), F32),
                pltpu.VMEM((4, length, half), BF16),
                pltpu.SemaphoreType.DMA((4 * tiles,)),
            ],
            [VMEM] * count + ([VMEM] * 2 + [HBM] * 4 if extra else []),
            out_specs,
            {count + 2 + index: index for index in range(4)} if extra else {},
            80 * length * width,
        )

    *partial, spectra, filter_blocks = results(
        0, [], [rows_out] * 4 + windows, [HBM] * 4 + [VMEM] * 2
    )
    final = results(1, [spectra, filter_blocks, *partial], [rows_out] * 4, [HBM] * 4)

    while step < chans:
        arrived = lax.ppermute(grad_filter, "chan", [(i, i ^ step) for i in range(chans)])
        if 2 * step < chans <= 4 * step:
            grad_filter = after(grad_filter, spectra)
        grad_filter = grad_filter + arrived
        step *= 2
    return (*final, grad_filter)


def solution(mesh):
    in_specs = (
        P("seq", "chan"),
        P("seq", "chan"),
        P("seq", "chan"),
        P(None, None, "chan"),
        P("seq", None),
        P("seq", "chan"),
    )
    out_specs = (
        P("seq", "chan"),
        P("seq", "chan"),
        P("seq", "chan"),
        P("seq", "chan"),
        P("seq", None),
    )
    return jax.shard_map(
        per_device, mesh=mesh, in_specs=in_specs, out_specs=out_specs, check_vma=False
    )
```

profile of v0, /device:TPU:0, one launch (start us, length us, event | category | flops | bytes accessed | tf_op | source)
XLA Modules:
  0.0 42.2 jit_solution(12666759073305093646)
XLA Ops:
  0.6 1.4 %shard_map.119 = (bf16[4,128,1024]{2,1,0:T(8,128)(2,1)S(1)}, bf16[16,1024]{1,0:T(8,128)(2,1)S(1)}, f32[3,3,1024]{2,1,0:T(4,128)S(1)}, f32[128,128]{1,0:T(8,128)S...) custom-call(bf16[128,1024]{1,0:T(8,128)(2,1)} %q_hbm.1, bf16[128,1024]{1,0:T(8,128)(2,1)} %k_hbm.1, ...), custom_call_target="tpu_custom_call" | custom-call | flops 1 | bytes 1 | tf_op jit(solution)/shard_map/pallas_call | solution.py:509
  2.1 1.1 %shard_map.120 = (bf16[544,1024]{1,0:T(8,128)(2,1)S(1)}, f32[3,128,1024]{2,1,0:T(8,128)S(1)}, bf16[256,512]{1,0:T(8,128)(2,1)S(1)}, bf16[320,512]{1,0:T(8,128)(2,1)S(1)}) custom-call(bf16[4,128,1024]{2,1,0:T(8,128)(2,1)S(1)} %get-tuple-element.37.rows_ref.refs_0_, f32[3,3,1024]{2,1,0:T(4,128)S(1)} %get-tuple-element.38.taps_ref.refs_1_, ...), custom_call_target="tpu_custom_call" | custom-call | flops 1 | bytes 1 | tf_op jit(solution)/shard_map/pallas_call | solution.py:509
  3.2 0.5 %collective-permute-start.2 = (bf16[544,1024]{1,0:T(8,128)(2,1)S(1)}, bf16[544,1024]{1,0:T(8,128)(2,1)S(1)}, u32[]{:S(2)}, u32[]{:S(2)}) collective-permute-start(bf16[544,1024]{1,0:T(8,128)(2,1)S(1)} %get-tuple-element.45.own_ref), channel_id=1, source_target_pairs={{0,8},{8,0},{16,24},{24,16},{1,9},{9,1},{17,25},{25,17},{2,10},{10... | collective-permute-start | bytes 3342344 | tf_op jit(solution)/shard_map/ppermute | solution.py:505
  3.7 2.6 %collective-permute-start = (bf16[16,1024]{1,0:T(8,128)(2,1)S(1)}, bf16[16,1024]{1,0:T(8,128)(2,1)S(1)}, u32[]{:S(2)}, u32[]{:S(2)}) collective-permute-start(bf16[16,1024]{1,0:T(8,128)(2,1)S(1)} %get-tuple-element.41.own_marks), channel_id=1, source_target_pairs={{0,16},{8,24},{16,0},{24,8},{1,17},{9,25},{17,1},{25,9},{2,18},{10... | collective-permute-start | bytes 98312 | tf_op jit(solution)/shard_map/ppermute | solution.py:505
  6.3 2.0 %collective-permute-done.refs_0_ = bf16[16,1024]{1,0:T(8,128)(2,1)S(1)} collective-permute-done((bf16[16,1024]{1,0:T(8,128)(2,1)S(1)}, bf16[16,1024]{1,0:T(8,128)(2,1)S(1)}, u32[]{:S(2)}, u32[]{:S(2)}) %collective-permute-start) | collective-permute-done | bytes 32800 | tf_op jit(solution)/shard_map/ppermute | solution.py:505
  8.3 1.9 %collective-permute-start.3 = (bf16[256,512]{1,0:T(8,128)(2,1)S(1)}, bf16[256,512]{1,0:T(8,128)(2,1)S(1)}, u32[]{:S(2)}, u32[]{:S(2)}) collective-permute-start(bf16[256,512]{1,0:T(8,128)(2,1)S(1)} %get-tuple-element.50), channel_id=1, source_target_pairs={{0,16},{8,24},{16,0},{24,8},{1,17},{9,25},{17,1},{25,9},{2,18},{10... | collective-permute-start | bytes 786440 | tf_op jit(solution)/shard_map/ppermute | solution.py:505
  10.2 0.2 collective-permute-start.4
  10.4 1.1 %collective-permute-done.1.refs_1_ = bf16[32,1024]{1,0:T(8,128)(2,1)S(1)} collective-permute-done((bf16[32,1024]{1,0:T(8,128)(2,1)S(1)}, bf16[32,1024]{1,0:T(8,128)(2,1)S(1)}, u32[]{:S(2)}, u32[]{:S(2)}) %collective-permute-start.1) | collective-permute-done | bytes 65568 | tf_op jit(solution)/shard_map/ppermute | solution.py:505
  11.5 0.4 shard_map.121
  11.9 2.4 %shard_map.122 = (f32[4,256,1024]{2,1,0:T(8,128)S(1)}, f32[2,256,128]{2,1,0:T(8,128)S(1)}) custom-call(bf16[544,1024]{1,0:T(8,128)(2,1)S(1)} %get-tuple-element.45.own_ref, bf16[544,1024]{1,0:T(8,128)(2,1)S(1)} %collective-permute-done.2.other_ref.refs_7_, f32[4,2,8,1024]{3,2,1,0:T(8,128)S(1)} %get-tuple-element.43.firsts_ref.refs_5_, ...), custom_call_target="tpu_custom_call" | custom-call | flops 1 | bytes 1 | tf_op jit(solution)/shard_map/pallas_call | solution.py:509
  14.2 3.2 %collective-permute-done.3.refs_0_.refs_11_ = bf16[256,512]{1,0:T(8,128)(2,1)S(1)} collective-permute-done((bf16[256,512]{1,0:T(8,128)(2,1)S(1)}, bf16[256,512]{1,0:T(8,128)(2,1)S(1)}, u32[]{:S(2)}, u32[]{:S(2)}) %collective-permute-start.3) | collective-permute-done | bytes 262176 | tf_op jit(solution)/shard_map/ppermute | solution.py:505
  17.5 1.3 %shard_map.123 = (f32[2,128,128]{2,1,0:T(8,128)S(1)}, f32[2,128,128]{2,1,0:T(8,128)S(1)}) custom-call(f32[4,256,1024]{2,1,0:T(8,128)S(1)} %get-tuple-element.47.spec_ref.refs_8_, f32[2,256,128]{2,1,0:T(8,128)S(1)} %get-tuple-element.52.near_ref, f32[4,2,8,1024]{3,2,1,0:T(8,128)S(1)} %get-tuple-element.43.firsts_ref.refs_5_, ...), custom_call_target="tpu_custom_call" | custom-call | flops 1 | bytes 1 | tf_op jit(solution)/shard_map/pallas_call | solution.py:509
  18.8 1.3 %collective-permute-done.5 = f32[2,128,128]{2,1,0:T(8,128)S(1)} collective-permute-done((f32[2,128,128]{2,1,0:T(8,128)S(1)}, f32[2,128,128]{2,1,0:T(8,128)S(1)}, u32[]{:S(2)}, u32[]{:S(2)}) %collective-permute-start.5) | collective-permute-done | bytes 131104 | tf_op jit(solution)/shard_map/ppermute | solution.py:505
  20.2 2.0 %collective-permute-start.6 = (f32[2,128,128]{2,1,0:T(8,128)S(1)}, f32[2,128,128]{2,1,0:T(8,128)S(1)}, u32[]{:S(2)}, u32[]{:S(2)}) collective-permute-start(f32[2,128,128]{2,1,0:T(8,128)S(1)} %add.15), channel_id=1, source_target_pairs={{0,1},{1,0},{2,3},{3,2},{4,5},{5,4},{6,7},{7,6},{8,9},{9,8},{10,11... | collective-permute-start | bytes 393224 | tf_op jit(solution)/shard_map/ppermute | solution.py:605
  22.2 3.8 %collective-permute-done.6 = f32[2,128,128]{2,1,0:T(8,128)S(1)} collective-permute-done((f32[2,128,128]{2,1,0:T(8,128)S(1)}, f32[2,128,128]{2,1,0:T(8,128)S(1)}, u32[]{:S(2)}, u32[]{:S(2)}) %collective-permute-start.6) | collective-permute-done | bytes 131104 | tf_op jit(solution)/shard_map/ppermute | solution.py:605
  26.1 1.8 %collective-permute-start.9 = (f32[1,128,128]{2,1,0:T(8,128)S(1)}, f32[1,128,128]{2,1,0:T(8,128)S(1)}, u32[]{:S(2)}, u32[]{:S(2)}) collective-permute-start(f32[1,128,128]{2,1,0:T(8,128)S(1)} %slice.9), channel_id=1, source_target_pairs={{0,16},{8,24},{16,0},{24,8},{1,17},{9,25},{17,1},{25,9},{2,18},{10... | collective-permute-start | bytes 196616 | tf_op jit(solution)/shard_map/ppermute | solution.py:505
  27.8 0.5 %collective-permute-start.7 = (bf16[256,512]{1,0:T(8,128)(2,1)S(1)}, bf16[256,512]{1,0:T(8,128)(2,1)S(1)}, u32[]{:S(2)}, u32[]{:S(2)}) collective-permute-start(bf16[256,512]{1,0:T(8,128)(2,1)S(1)} %collective-permute-done.3.refs_0_.refs_11_), channel_id=1, source_target_pairs={{0,8},{8,0},{16,24},{24,16},{1,9},{9,1},{17,25},{25,17},{2,10},{10... | collective-permute-start | bytes 786440 | tf_op jit(solution)/shard_map/ppermute | solution.py:505
  28.4 2.0 %collective-permute-done.9 = f32[1,128,128]{2,1,0:T(8,128)S(1)} collective-permute-done((f32[1,128,128]{2,1,0:T(8,128)S(1)}, f32[1,128,128]{2,1,0:T(8,128)S(1)}, u32[]{:S(2)}, u32[]{:S(2)}) %collective-permute-start.9) | collective-permute-done | bytes 65568 | tf_op jit(solution)/shard_map/ppermute | solution.py:505
  30.4 1.9 %collective-permute-start.10 = (f32[128,128]{1,0:T(8,128)S(1)}, f32[128,128]{1,0:T(8,128)S(1)}, u32[]{:S(2)}, u32[]{:S(2)}) collective-permute-start(f32[128,128]{1,0:T(8,128)S(1)} %add_bitcast_fusion), channel_id=1, source_target_pairs={{0,2},{1,3},{2,0},{3,1},{4,6},{5,7},{6,4},{7,5},{8,10},{9,11},{10,... | collective-permute-start | bytes 196616 | tf_op jit(solution)/shard_map/ppermute | solution.py:649
  32.3 3.3 %shard_map.124 = (bf16[128,1024]{1,0:T(8,128)(2,1)}, bf16[128,1024]{1,0:T(8,128)(2,1)}, bf16[128,1024]{1,0:T(8,128)(2,1)}, bf16[128,1024]{1,0:T(8,128)(2,1)}, f3...) custom-call(bf16[4,128,1024]{2,1,0:T(8,128)(2,1)S(1)} %get-tuple-element.37.rows_ref.refs_0_, ...), custom_call_target="tpu_custom_call" | custom-call | flops 1 | bytes 10485760 | tf_op jit(solution)/shard_map/pallas_call | solution.py:509
  35.7 2.6 %collective-permute-start.11 = (f32[128,128]{1,0:T(8,128)S(1)}, f32[128,128]{1,0:T(8,128)S(1)}, u32[]{:S(2)}, u32[]{:S(2)}) collective-permute-start(f32[128,128]{1,0:T(8,128)S(1)} %add.18), channel_id=1, source_target_pairs={{0,4},{1,5},{2,6},{3,7},{4,0},{5,1},{6,2},{7,3},{8,12},{9,13},{10,... | collective-permute-start | bytes 196616 | tf_op jit(solution)/shard_map/ppermute | solution.py:649
  38.3 3.0 %shard_map.125 = (bf16[128,1024]{1,0:T(8,128)(2,1)}, bf16[128,1024]{1,0:T(8,128)(2,1)}, bf16[128,1024]{1,0:T(8,128)(2,1)}, bf16[128,1024]{1,0:T(8,128)(2,1)}) custom-call(bf16[4,128,1024]{2,1,0:T(8,128)(2,1)S(1)} %get-tuple-element.37.rows_ref.refs_0_, ...), custom_call_target="tpu_custom_call", output_to_operand_aliasing={{0}: (17, {}), {1}: (18, {}), {2}: (19, {}), {3}: (20, {})} | custom-call | flops 1 | bytes 10485760 | tf_op jit(solution)/shard_map/pallas_call | solution.py:509
  41.3 0.3 collective-permute-done.11
  41.6 0.6 %add.19 = f32[128,128]{1,0:T(8,128)} add(f32[128,128]{1,0:T(8,128)S(1)} %add.18, f32[128,128]{1,0:T(8,128)S(1)} %collective-permute-done.11) | non-fusion elementwise | flops 16384 | bytes 196608 | tf_op jit(solution)/shard_map/add | solution.py:652
  (14 shorter events, 0.2 us)
Async XLA Ops:
  3.2 8.7 %collective-permute-start.2 = (bf16[544,1024]{1,0:T(8,128)(2,1)S(1)}, bf16[544,1024]{1,0:T(8,128)(2,1)S(1)}, u32[]{:S(2)}, u32[]{:S(2)}) collective-permute-start(bf16[544,1024]{1,0:T(8,128)(2,1)S(1)} %get-tuple-element.45.own_ref), channel_id=1, source_target_pairs={{0,8},{8,0},{16,24},{24,16},{1,9},{9,1},{17,25},{25,17},{2,10},{10... | collective-permute-start | bytes 3342344 | tf_op jit(solution)/shard_map/ppermute | solution.py:505
  3.7 4.6 %collective-permute-start = (bf16[16,1024]{1,0:T(8,128)(2,1)S(1)}, bf16[16,1024]{1,0:T(8,128)(2,1)S(1)}, u32[]{:S(2)}, u32[]{:S(2)}) collective-permute-start(bf16[16,1024]{1,0:T(8,128)(2,1)S(1)} %get-tuple-element.41.own_marks), channel_id=1, source_target_pairs={{0,16},{8,24},{16,0},{24,8},{1,17},{9,25},{17,1},{25,9},{2,18},{10... | collective-permute-start | bytes 98312 | tf_op jit(solution)/shard_map/ppermute | solution.py:505
  8.3 9.2 %collective-permute-start.3 = (bf16[256,512]{1,0:T(8,128)(2,1)S(1)}, bf16[256,512]{1,0:T(8,128)(2,1)S(1)}, u32[]{:S(2)}, u32[]{:S(2)}) collective-permute-start(bf16[256,512]{1,0:T(8,128)(2,1)S(1)} %get-tuple-element.50), channel_id=1, source_target_pairs={{0,16},{8,24},{16,0},{24,8},{1,17},{9,25},{17,1},{25,9},{2,18},{10... | collective-permute-start | bytes 786440 | tf_op jit(solution)/shard_map/ppermute | solution.py:505
  10.2 1.3 %collective-permute-start.1 = (bf16[32,1024]{1,0:T(8,128)(2,1)S(1)}, bf16[32,1024]{1,0:T(8,128)(2,1)S(1)}, u32[]{:S(2)}, u32[]{:S(2)}) collective-permute-start(bf16[32,1024]{1,0:T(8,128)(2,1)S(1)} %pad_maximum_fusion), channel_id=1, source_target_pairs={{0,8},{8,0},{16,24},{24,16},{1,9},{9,1},{17,25},{25,17},{2,10},{10... | collective-permute-start | bytes 196616 | tf_op jit(solution)/shard_map/ppermute | solution.py:505
  10.2 15.8 %collective-permute-start.4 = (bf16[320,512]{1,0:T(8,128)(2,1)S(1)}, bf16[320,512]{1,0:T(8,128)(2,1)S(1)}, u32[]{:S(2)}, u32[]{:S(2)}) collective-permute-start(bf16[320,512]{1,0:T(8,128)(2,1)S(1)} %get-tuple-element.51), channel_id=1, source_target_pairs={{0,16},{8,24},{16,0},{24,8},{1,17},{9,25},{17,1},{25,9},{2,18},{10... | collective-permute-start | bytes 983048 | tf_op jit(solution)/shard_map/ppermute | solution.py:505
  18.7 1.4 %collective-permute-start.5 = (f32[2,128,128]{2,1,0:T(8,128)S(1)}, f32[2,128,128]{2,1,0:T(8,128)S(1)}, u32[]{:S(2)}, u32[]{:S(2)}) collective-permute-start(f32[2,128,128]{2,1,0:T(8,128)S(1)} %get-tuple-element.54), channel_id=1, source_target_pairs={{0,8},{8,0},{16,24},{24,16},{1,9},{9,1},{17,25},{25,17},{2,10},{10... | collective-permute-start | bytes 393224 | tf_op jit(solution)/shard_map/ppermute | solution.py:505
  20.2 5.8 %collective-permute-start.6 = (f32[2,128,128]{2,1,0:T(8,128)S(1)}, f32[2,128,128]{2,1,0:T(8,128)S(1)}, u32[]{:S(2)}, u32[]{:S(2)}) collective-permute-start(f32[2,128,128]{2,1,0:T(8,128)S(1)} %add.15), channel_id=1, source_target_pairs={{0,1},{1,0},{2,3},{3,2},{4,5},{5,4},{6,7},{7,6},{8,9},{9,8},{10,11... | collective-permute-start | bytes 393224 | tf_op jit(solution)/shard_map/ppermute | solution.py:605
  26.1 4.3 %collective-permute-start.9 = (f32[1,128,128]{2,1,0:T(8,128)S(1)}, f32[1,128,128]{2,1,0:T(8,128)S(1)}, u32[]{:S(2)}, u32[]{:S(2)}) collective-permute-start(f32[1,128,128]{2,1,0:T(8,128)S(1)} %slice.9), channel_id=1, source_target_pairs={{0,16},{8,24},{16,0},{24,8},{1,17},{9,25},{17,1},{25,9},{2,18},{10... | collective-permute-start | bytes 196616 | tf_op jit(solution)/shard_map/ppermute | solution.py:505
  27.8 4.5 %collective-permute-start.8 = (bf16[320,512]{1,0:T(8,128)(2,1)S(1)}, bf16[320,512]{1,0:T(8,128)(2,1)S(1)}, u32[]{:S(2)}, u32[]{:S(2)}) collective-permute-start(bf16[320,512]{1,0:T(8,128)(2,1)S(1)} %collective-permute-done.4.refs_12_), channel_id=1, source_target_pairs={{0,8},{8,0},{16,24},{24,16},{1,9},{9,1},{17,25},{25,17},{2,10},{10... | collective-permute-start | bytes 983048 | tf_op jit(solution)/shard_map/ppermute | solution.py:505
  27.8 4.5 %collective-permute-start.7 = (bf16[256,512]{1,0:T(8,128)(2,1)S(1)}, bf16[256,512]{1,0:T(8,128)(2,1)S(1)}, u32[]{:S(2)}, u32[]{:S(2)}) collective-permute-start(bf16[256,512]{1,0:T(8,128)(2,1)S(1)} %collective-permute-done.3.refs_0_.refs_11_), channel_id=1, source_target_pairs={{0,8},{8,0},{16,24},{24,16},{1,9},{9,1},{17,25},{25,17},{2,10},{10... | collective-permute-start | bytes 786440 | tf_op jit(solution)/shard_map/ppermute | solution.py:505
  30.4 5.2 %collective-permute-start.10 = (f32[128,128]{1,0:T(8,128)S(1)}, f32[128,128]{1,0:T(8,128)S(1)}, u32[]{:S(2)}, u32[]{:S(2)}) collective-permute-start(f32[128,128]{1,0:T(8,128)S(1)} %add_bitcast_fusion), channel_id=1, source_target_pairs={{0,2},{1,3},{2,0},{3,1},{4,6},{5,7},{6,4},{7,5},{8,10},{9,11},{10,... | collective-permute-start | bytes 196616 | tf_op jit(solution)/shard_map/ppermute | solution.py:649
  35.7 5.9 %collective-permute-start.11 = (f32[128,128]{1,0:T(8,128)S(1)}, f32[128,128]{1,0:T(8,128)S(1)}, u32[]{:S(2)}, u32[]{:S(2)}) collective-permute-start(f32[128,128]{1,0:T(8,128)S(1)} %add.18), channel_id=1, source_target_pairs={{0,4},{1,5},{2,6},{3,7},{4,0},{5,1},{6,2},{7,3},{8,12},{9,13},{10,... | collective-permute-start | bytes 196616 | tf_op jit(solution)/shard_map/ppermute | solution.py:649
where the time goes:
time: 42.4 us; the launch traced here: 42.2 us
  starting transfers between devices  14.1 us (33%)
  waiting for transfers between devices  13.8 us (33%)
  Pallas kernels  12.9 us (30%)
  between operations  0.75 us (2%)
  other arithmetic  0.69 us (2%)
    pallas_call x7, Pallas kernels, call(): pl.pallas_call(kernel, out_shape=outs, in_specs=in_specs or [VMEM] * len(...  12.9 us
    ppermute x9, waiting for transfers between devices, swap(): return lax.ppermute(block, 'seq', [(i, i ^ bit) for i in range(blocks)])  9.69 us
    ppermute x9, starting transfers between devices, swap(): return lax.ppermute(block, 'seq', [(i, i ^ bit) for i in range(blocks)])  7.56 us
    ppermute x2, starting transfers between devices, per_device(): lax.ppermute(grad_filter, 'chan', [(i, i ^ step) for i in range(chans)])  4.54 us
    ppermute x1, waiting for transfers between devices, per_device(): even = even + lax.ppermute(even, 'chan', [(i, i ^ 1) for i in range(chans)])  3.81 us
    ppermute x1, starting transfers between devices, per_device(): even = even + lax.ppermute(even, 'chan', [(i, i ^ 1) for i in range(chans)])  2.03 us
  transfers between devices with their start and end apart: 12, of which 7 were waited for; matrix products, arithmetic and copies ran while one was open for 0% of the time, Pallas kernels for 24%

commit v1 on v0

--- a/solution.py
+++ b/solution.py
@@ -573,6 +573,7 @@
         [pair_shape, shape((3, length, width), F32)] + [first_shape, later_shape] * len(bits),
         [rows, short_taps, long_filter],
         [pltpu.VMEM((3, EDGE + length, tile_width), F32)],
+        cost=40 * length * width,
     )
 
     def gather(own):
@@ -586,7 +587,6 @@
 
     firsts = gather([after(unit, all_marks[0]) for unit in own_units[0::2]])
     sibling = swap(pair, 1)
-    laters = gather(own_units[1::2])
     spec, near = call(
         functools.partial(chip_kernel, tile_width, groups, margin),
         [shape((4, 2 * length, width), F32), shape((2, 2 * length, groups), F32)],
@@ -599,6 +599,7 @@
         [spec, near, firsts_true, forward, inverse, *firsts],
         [pltpu.VMEM((blocks + 1, 2 * length, groups), F32)],
     )
+    laters = gather([after(unit, near) for unit in own_units[1::2]])
     even = even + swap(odd, 1)
     step = 1
     if chans > 1:

time: 42.4 us -> 40.6 us (0.958)
  starting transfers between devices: 14.1 us -> 13.1 us
  waiting for transfers between devices: 13.8 us -> 13.1 us
    ppermute x9, waiting for transfers between devices: 9.69 us -> 8.63 us  [swap(): return lax.ppermute(block, 'seq', [(i, i ^ bit) for i in range(blocks)])]
    ppermute x1, starting transfers between devices: 2.03 us -> 1.43 us  [per_device(): even = even + lax.ppermute(even, 'chan', [(i, i ^ 1) for i in range(chans)])]
  transfers between devices with their start and end apart: 12 -> 12, of which waited for: 7 -> 7; matrix products, arithmetic and copies ran while one was open for 0% -> 0% of each run, Pallas kernels for 24% -> 25%
where the time goes in v1:
time: 40.6 us; the launch traced here: 40.5 us
  starting transfers between devices  13.1 us (32%)
  waiting for transfers between devices  13.1 us (32%)
  Pallas kernels  12.8 us (32%)
  between operations  0.75 us (2%)
  other arithmetic  0.7 us (2%)
    pallas_call x7, Pallas kernels, call(): pl.pallas_call(kernel, out_shape=outs, in_specs=in_specs or [VMEM] * len(...  12.8 us
    ppermute x9, waiting for transfers between devices, swap(): return lax.ppermute(block, 'seq', [(i, i ^ bit) for i in range(blocks)])  8.63 us
    ppermute x9, starting transfers between devices, swap(): return lax.ppermute(block, 'seq', [(i, i ^ bit) for i in range(blocks)])  7.5 us
    ppermute x1, waiting for transfers between devices, per_device(): even = even + lax.ppermute(even, 'chan', [(i, i ^ 1) for i in range(chans)])  4.19 us
    ppermute x2, starting transfers between devices, per_device(): lax.ppermute(grad_filter, 'chan', [(i, i ^ step) for i in range(chans)])  4.16 us
    ppermute x1, starting transfers between devices, per_device(): even = even + lax.ppermute(even, 'chan', [(i, i ^ 1) for i in range(chans)])  1.43 us
  transfers between devices with their start and end apart: 12, of which 7 were waited for; matrix products, arithmetic and copies ran while one was open for 0% of the time, Pallas kernels for 25%

profile of v1, /device:TPU:0, one launch (start us, length us, event | category | flops | bytes accessed | tf_op | source)
XLA Modules:
  0.0 40.5 jit_solution(5096288323767519904)
XLA Ops:
  0.6 1.4 %shard_map.119 = (bf16[4,128,1024]{2,1,0:T(8,128)(2,1)S(1)}, bf16[16,1024]{1,0:T(8,128)(2,1)S(1)}, f32[3,3,1024]{2,1,0:T(4,128)S(1)}, f32[128,128]{1,0:T(8,128)S...) custom-call(bf16[128,1024]{1,0:T(8,128)(2,1)} %q_hbm.1, bf16[128,1024]{1,0:T(8,128)(2,1)} %k_hbm.1, ...), custom_call_target="tpu_custom_call" | custom-call | flops 1 | bytes 1 | tf_op jit(solution)/shard_map/pallas_call | solution.py:509
  2.1 1.1 %shard_map.120 = (bf16[544,1024]{1,0:T(8,128)(2,1)S(1)}, f32[3,128,1024]{2,1,0:T(8,128)S(1)}, bf16[256,512]{1,0:T(8,128)(2,1)S(1)}, bf16[320,512]{1,0:T(8,128)(2,1)S(1)}) custom-call(bf16[4,128,1024]{2,1,0:T(8,128)(2,1)S(1)} %get-tuple-element.38.rows_ref.refs_0_, f32[3,3,1024]{2,1,0:T(4,128)S(1)} %get-tuple-element.39.taps_ref.refs_1_, ...), custom_call_target="tpu_custom_call" | custom-call | flops 1 | bytes 5242880 | tf_op jit(solution)/shard_map/pallas_call | solution.py:509
  3.2 0.5 %collective-permute-start.2 = (bf16[544,1024]{1,0:T(8,128)(2,1)S(1)}, bf16[544,1024]{1,0:T(8,128)(2,1)S(1)}, u32[]{:S(2)}, u32[]{:S(2)}) collective-permute-start(bf16[544,1024]{1,0:T(8,128)(2,1)S(1)} %get-tuple-element.46.own_ref), channel_id=1, source_target_pairs={{0,8},{8,0},{16,24},{24,16},{1,9},{9,1},{17,25},{25,17},{2,10},{10... | collective-permute-start | bytes 3342344 | tf_op jit(solution)/shard_map/ppermute | solution.py:505
  3.7 2.6 %collective-permute-start = (bf16[16,1024]{1,0:T(8,128)(2,1)S(1)}, bf16[16,1024]{1,0:T(8,128)(2,1)S(1)}, u32[]{:S(2)}, u32[]{:S(2)}) collective-permute-start(bf16[16,1024]{1,0:T(8,128)(2,1)S(1)} %get-tuple-element.42.own_marks), channel_id=1, source_target_pairs={{0,16},{8,24},{16,0},{24,8},{1,17},{9,25},{17,1},{25,9},{2,18},{10... | collective-permute-start | bytes 98312 | tf_op jit(solution)/shard_map/ppermute | solution.py:505
  6.3 2.0 %collective-permute-done.refs_0_ = bf16[16,1024]{1,0:T(8,128)(2,1)S(1)} collective-permute-done((bf16[16,1024]{1,0:T(8,128)(2,1)S(1)}, bf16[16,1024]{1,0:T(8,128)(2,1)S(1)}, u32[]{:S(2)}, u32[]{:S(2)}) %collective-permute-start) | collective-permute-done | bytes 32800 | tf_op jit(solution)/shard_map/ppermute | solution.py:505
  8.3 1.9 %collective-permute-start.3 = (bf16[256,512]{1,0:T(8,128)(2,1)S(1)}, bf16[256,512]{1,0:T(8,128)(2,1)S(1)}, u32[]{:S(2)}, u32[]{:S(2)}) collective-permute-start(bf16[256,512]{1,0:T(8,128)(2,1)S(1)} %get-tuple-element.51), channel_id=1, source_target_pairs={{0,16},{8,24},{16,0},{24,8},{1,17},{9,25},{17,1},{25,9},{2,18},{10... | collective-permute-start | bytes 786440 | tf_op jit(solution)/shard_map/ppermute | solution.py:505
  10.2 1.2 %collective-permute-done.1.refs_1_ = bf16[32,1024]{1,0:T(8,128)(2,1)S(1)} collective-permute-done((bf16[32,1024]{1,0:T(8,128)(2,1)S(1)}, bf16[32,1024]{1,0:T(8,128)(2,1)S(1)}, u32[]{:S(2)}, u32[]{:S(2)}) %collective-permute-start.1) | collective-permute-done | bytes 65568 | tf_op jit(solution)/shard_map/ppermute | solution.py:505
  11.5 0.4 shard_map.121
  11.9 2.4 %shard_map.122 = (f32[4,256,1024]{2,1,0:T(8,128)S(1)}, f32[2,256,128]{2,1,0:T(8,128)S(1)}) custom-call(bf16[544,1024]{1,0:T(8,128)(2,1)S(1)} %get-tuple-element.46.own_ref, bf16[544,1024]{1,0:T(8,128)(2,1)S(1)} %collective-permute-done.2.other_ref.refs_7_, f32[4,2,8,1024]{3,2,1,0:T(8,128)S(1)} %get-tuple-element.44.firsts_ref.refs_5_, ...), custom_call_target="tpu_custom_call" | custom-call | flops 1 | bytes 1 | tf_op jit(solution)/shard_map/pallas_call | solution.py:509
  14.2 0.2 collective-permute-start.4
  14.4 2.0 %collective-permute-done.3.refs_0_.refs_11_ = bf16[256,512]{1,0:T(8,128)(2,1)S(1)} collective-permute-done((bf16[256,512]{1,0:T(8,128)(2,1)S(1)}, bf16[256,512]{1,0:T(8,128)(2,1)S(1)}, u32[]{:S(2)}, u32[]{:S(2)}) %collective-permute-start.3) | collective-permute-done | bytes 262176 | tf_op jit(solution)/shard_map/ppermute | solution.py:505
  16.3 1.3 %shard_map.123 = (f32[2,128,128]{2,1,0:T(8,128)S(1)}, f32[2,128,128]{2,1,0:T(8,128)S(1)}) custom-call(f32[4,256,1024]{2,1,0:T(8,128)S(1)} %get-tuple-element.48.spec_ref.refs_8_, f32[2,256,128]{2,1,0:T(8,128)S(1)} %get-tuple-element.53.near_ref, f32[4,2,8,1024]{3,2,1,0:T(8,128)S(1)} %get-tuple-element.44.firsts_ref.refs_5_, ...), custom_call_target="tpu_custom_call" | custom-call | flops 1 | bytes 1 | tf_op jit(solution)/shard_map/pallas_call | solution.py:509
  17.7 1.3 %collective-permute-done.5 = f32[2,128,128]{2,1,0:T(8,128)S(1)} collective-permute-done((f32[2,128,128]{2,1,0:T(8,128)S(1)}, f32[2,128,128]{2,1,0:T(8,128)S(1)}, u32[]{:S(2)}, u32[]{:S(2)}) %collective-permute-start.5) | collective-permute-done | bytes 131104 | tf_op jit(solution)/shard_map/ppermute | solution.py:505
  19.0 1.4 %collective-permute-start.6 = (f32[2,128,128]{2,1,0:T(8,128)S(1)}, f32[2,128,128]{2,1,0:T(8,128)S(1)}, u32[]{:S(2)}, u32[]{:S(2)}) collective-permute-start(f32[2,128,128]{2,1,0:T(8,128)S(1)} %add.15), channel_id=1, source_target_pairs={{0,1},{1,0},{2,3},{3,2},{4,5},{5,4},{6,7},{7,6},{8,9},{9,8},{10,11... | collective-permute-start | bytes 393224 | tf_op jit(solution)/shard_map/ppermute | solution.py:606
  20.5 4.2 %collective-permute-done.6 = f32[2,128,128]{2,1,0:T(8,128)S(1)} collective-permute-done((f32[2,128,128]{2,1,0:T(8,128)S(1)}, f32[2,128,128]{2,1,0:T(8,128)S(1)}, u32[]{:S(2)}, u32[]{:S(2)}) %collective-permute-start.6) | collective-permute-done | bytes 131104 | tf_op jit(solution)/shard_map/ppermute | solution.py:606
  24.7 1.7 %collective-permute-start.9 = (f32[1,128,128]{2,1,0:T(8,128)S(1)}, f32[1,128,128]{2,1,0:T(8,128)S(1)}, u32[]{:S(2)}, u32[]{:S(2)}) collective-permute-start(f32[1,128,128]{2,1,0:T(8,128)S(1)} %slice.9), channel_id=1, source_target_pairs={{0,16},{8,24},{16,0},{24,8},{1,17},{9,25},{17,1},{25,9},{2,18},{10... | collective-permute-start | bytes 196616 | tf_op jit(solution)/shard_map/ppermute | solution.py:505
  26.4 0.5 %collective-permute-start.7 = (bf16[256,512]{1,0:T(8,128)(2,1)S(1)}, bf16[256,512]{1,0:T(8,128)(2,1)S(1)}, u32[]{:S(2)}, u32[]{:S(2)}) collective-permute-start(bf16[256,512]{1,0:T(8,128)(2,1)S(1)} %collective-permute-done.3.refs_0_.refs_11_), channel_id=1, source_target_pairs={{0,8},{8,0},{16,24},{24,16},{1,9},{9,1},{17,25},{25,17},{2,10},{10... | collective-permute-start | bytes 786440 | tf_op jit(solution)/shard_map/ppermute | solution.py:505
  26.9 2.1 %collective-permute-done.9 = f32[1,128,128]{2,1,0:T(8,128)S(1)} collective-permute-done((f32[1,128,128]{2,1,0:T(8,128)S(1)}, f32[1,128,128]{2,1,0:T(8,128)S(1)}, u32[]{:S(2)}, u32[]{:S(2)}) %collective-permute-start.9) | collective-permute-done | bytes 65568 | tf_op jit(solution)/shard_map/ppermute | solution.py:505
  29.0 1.5 %collective-permute-start.10 = (f32[128,128]{1,0:T(8,128)S(1)}, f32[128,128]{1,0:T(8,128)S(1)}, u32[]{:S(2)}, u32[]{:S(2)}) collective-permute-start(f32[128,128]{1,0:T(8,128)S(1)} %add_bitcast_fusion), channel_id=1, source_target_pairs={{0,2},{1,3},{2,0},{3,1},{4,6},{5,7},{6,4},{7,5},{8,10},{9,11},{10,... | collective-permute-start | bytes 196616 | tf_op jit(solution)/shard_map/ppermute | solution.py:650
  30.6 3.3 %shard_map.124 = (bf16[128,1024]{1,0:T(8,128)(2,1)}, bf16[128,1024]{1,0:T(8,128)(2,1)}, bf16[128,1024]{1,0:T(8,128)(2,1)}, bf16[128,1024]{1,0:T(8,128)(2,1)}, f3...) custom-call(bf16[4,128,1024]{2,1,0:T(8,128)(2,1)S(1)} %get-tuple-element.38.rows_ref.refs_0_, ...), custom_call_target="tpu_custom_call" | custom-call | flops 1 | bytes 10485760 | tf_op jit(solution)/shard_map/pallas_call | solution.py:509
  33.9 2.7 %collective-permute-start.11 = (f32[128,128]{1,0:T(8,128)S(1)}, f32[128,128]{1,0:T(8,128)S(1)}, u32[]{:S(2)}, u32[]{:S(2)}) collective-permute-start(f32[128,128]{1,0:T(8,128)S(1)} %add.18), channel_id=1, source_target_pairs={{0,4},{1,5},{2,6},{3,7},{4,0},{5,1},{6,2},{7,3},{8,12},{9,13},{10,... | collective-permute-start | bytes 196616 | tf_op jit(solution)/shard_map/ppermute | solution.py:650
  36.6 3.0 %shard_map.125 = (bf16[128,1024]{1,0:T(8,128)(2,1)}, bf16[128,1024]{1,0:T(8,128)(2,1)}, bf16[128,1024]{1,0:T(8,128)(2,1)}, bf16[128,1024]{1,0:T(8,128)(2,1)}) custom-call(bf16[4,128,1024]{2,1,0:T(8,128)(2,1)S(1)} %get-tuple-element.38.rows_ref.refs_0_, ...), custom_call_target="tpu_custom_call", output_to_operand_aliasing={{0}: (17, {}), {1}: (18, {}), {2}: (19, {}), {3}: (20, {})} | custom-call | flops 1 | bytes 10485760 | tf_op jit(solution)/shard_map/pallas_call | solution.py:509
  39.5 0.3 collective-permute-done.11
  39.8 0.6 %add.19 = f32[128,128]{1,0:T(8,128)} add(f32[128,128]{1,0:T(8,128)S(1)} %add.18, f32[128,128]{1,0:T(8,128)S(1)} %collective-permute-done.11) | non-fusion elementwise | flops 16384 | bytes 196608 | tf_op jit(solution)/shard_map/add | solution.py:653
  (14 shorter events, 0.2 us)
Async XLA Ops:
  3.2 8.7 %collective-permute-start.2 = (bf16[544,1024]{1,0:T(8,128)(2,1)S(1)}, bf16[544,1024]{1,0:T(8,128)(2,1)S(1)}, u32[]{:S(2)}, u32[]{:S(2)}) collective-permute-start(bf16[544,1024]{1,0:T(8,128)(2,1)S(1)} %get-tuple-element.46.own_ref), channel_id=1, source_target_pairs={{0,8},{8,0},{16,24},{24,16},{1,9},{9,1},{17,25},{25,17},{2,10},{10... | collective-permute-start | bytes 3342344 | tf_op jit(solution)/shard_map/ppermute | solution.py:505
  3.7 4.6 %collective-permute-start = (bf16[16,1024]{1,0:T(8,128)(2,1)S(1)}, bf16[16,1024]{1,0:T(8,128)(2,1)S(1)}, u32[]{:S(2)}, u32[]{:S(2)}) collective-permute-start(bf16[16,1024]{1,0:T(8,128)(2,1)S(1)} %get-tuple-element.42.own_marks), channel_id=1, source_target_pairs={{0,16},{8,24},{16,0},{24,8},{1,17},{9,25},{17,1},{25,9},{2,18},{10... | collective-permute-start | bytes 98312 | tf_op jit(solution)/shard_map/ppermute | solution.py:505
  8.3 8.1 %collective-permute-start.3 = (bf16[256,512]{1,0:T(8,128)(2,1)S(1)}, bf16[256,512]{1,0:T(8,128)(2,1)S(1)}, u32[]{:S(2)}, u32[]{:S(2)}) collective-permute-start(bf16[256,512]{1,0:T(8,128)(2,1)S(1)} %get-tuple-element.51), channel_id=1, source_target_pairs={{0,16},{8,24},{16,0},{24,8},{1,17},{9,25},{17,1},{25,9},{2,18},{10... | collective-permute-start | bytes 786440 | tf_op jit(solution)/shard_map/ppermute | solution.py:505
  10.2 1.3 %collective-permute-start.1 = (bf16[32,1024]{1,0:T(8,128)(2,1)S(1)}, bf16[32,1024]{1,0:T(8,128)(2,1)S(1)}, u32[]{:S(2)}, u32[]{:S(2)}) collective-permute-start(bf16[32,1024]{1,0:T(8,128)(2,1)S(1)} %pad_maximum_fusion), channel_id=1, source_target_pairs={{0,8},{8,0},{16,24},{24,16},{1,9},{9,1},{17,25},{25,17},{2,10},{10... | collective-permute-start | bytes 196616 | tf_op jit(solution)/shard_map/ppermute | solution.py:505
  14.2 10.5 %collective-permute-start.4 = (bf16[320,512]{1,0:T(8,128)(2,1)S(1)}, bf16[320,512]{1,0:T(8,128)(2,1)S(1)}, u32[]{:S(2)}, u32[]{:S(2)}) collective-permute-start(bf16[320,512]{1,0:T(8,128)(2,1)S(1)} %get-tuple-element.54), channel_id=1, source_target_pairs={{0,16},{8,24},{16,0},{24,8},{1,17},{9,25},{17,1},{25,9},{2,18},{10... | collective-permute-start | bytes 983048 | tf_op jit(solution)/shard_map/ppermute | solution.py:505
  17.6 1.4 %collective-permute-start.5 = (f32[2,128,128]{2,1,0:T(8,128)S(1)}, f32[2,128,128]{2,1,0:T(8,128)S(1)}, u32[]{:S(2)}, u32[]{:S(2)}) collective-permute-start(f32[2,128,128]{2,1,0:T(8,128)S(1)} %get-tuple-element.56), channel_id=1, source_target_pairs={{0,8},{8,0},{16,24},{24,16},{1,9},{9,1},{17,25},{25,17},{2,10},{10... | collective-permute-start | bytes 393224 | tf_op jit(solution)/shard_map/ppermute | solution.py:505
  19.0 5.6 %collective-permute-start.6 = (f32[2,128,128]{2,1,0:T(8,128)S(1)}, f32[2,128,128]{2,1,0:T(8,128)S(1)}, u32[]{:S(2)}, u32[]{:S(2)}) collective-permute-start(f32[2,128,128]{2,1,0:T(8,128)S(1)} %add.15), channel_id=1, source_target_pairs={{0,1},{1,0},{2,3},{3,2},{4,5},{5,4},{6,7},{7,6},{8,9},{9,8},{10,11... | collective-permute-start | bytes 393224 | tf_op jit(solution)/shard_map/ppermute | solution.py:606
  24.7 4.3 %collective-permute-start.9 = (f32[1,128,128]{2,1,0:T(8,128)S(1)}, f32[1,128,128]{2,1,0:T(8,128)S(1)}, u32[]{:S(2)}, u32[]{:S(2)}) collective-permute-start(f32[1,128,128]{2,1,0:T(8,128)S(1)} %slice.9), channel_id=1, source_target_pairs={{0,16},{8,24},{16,0},{24,8},{1,17},{9,25},{17,1},{25,9},{2,18},{10... | collective-permute-start | bytes 196616 | tf_op jit(solution)/shard_map/ppermute | solution.py:505
  26.4 4.1 %collective-permute-start.8 = (bf16[320,512]{1,0:T(8,128)(2,1)S(1)}, bf16[320,512]{1,0:T(8,128)(2,1)S(1)}, u32[]{:S(2)}, u32[]{:S(2)}) collective-permute-start(bf16[320,512]{1,0:T(8,128)(2,1)S(1)} %collective-permute-done.4.refs_12_), channel_id=1, source_target_pairs={{0,8},{8,0},{16,24},{24,16},{1,9},{9,1},{17,25},{25,17},{2,10},{10... | collective-permute-start | bytes 983048 | tf_op jit(solution)/shard_map/ppermute | solution.py:505
  26.4 4.1 %collective-permute-start.7 = (bf16[256,512]{1,0:T(8,128)(2,1)S(1)}, bf16[256,512]{1,0:T(8,128)(2,1)S(1)}, u32[]{:S(2)}, u32[]{:S(2)}) collective-permute-start(bf16[256,512]{1,0:T(8,128)(2,1)S(1)} %collective-permute-done.3.refs_0_.refs_11_), channel_id=1, source_target_pairs={{0,8},{8,0},{16,24},{24,16},{1,9},{9,1},{17,25},{25,17},{2,10},{10... | collective-permute-start | bytes 786440 | tf_op jit(solution)/shard_map/ppermute | solution.py:505
  29.0 4.8 %collective-permute-start.10 = (f32[128,128]{1,0:T(8,128)S(1)}, f32[128,128]{1,0:T(8,128)S(1)}, u32[]{:S(2)}, u32[]{:S(2)}) collective-permute-start(f32[128,128]{1,0:T(8,128)S(1)} %add_bitcast_fusion), channel_id=1, source_target_pairs={{0,2},{1,3},{2,0},{3,1},{4,6},{5,7},{6,4},{7,5},{8,10},{9,11},{10,... | collective-permute-start | bytes 196616 | tf_op jit(solution)/shard_map/ppermute | solution.py:650
  33.9 5.9 %collective-permute-start.11 = (f32[128,128]{1,0:T(8,128)S(1)}, f32[128,128]{1,0:T(8,128)S(1)}, u32[]{:S(2)}, u32[]{:S(2)}) collective-permute-start(f32[128,128]{1,0:T(8,128)S(1)} %add.18), channel_id=1, source_target_pairs={{0,4},{1,5},{2,6},{3,7},{4,0},{5,1},{6,2},{7,3},{8,12},{9,13},{10,... | collective-permute-start | bytes 196616 | tf_op jit(solution)/shard_map/ppermute | solution.py:650
